TPU v7x, 512 devices: a whole 4x8x8 slice. The times are simulated.
512 devices in a mesh: row: 32 (over x, z), col: 16 (over y, core).
Axes of the slice: x: 4, y: 8, z: 8, core: 2. Of those that a mesh axis runs over, the one named last changes fastest.
Arguments:
- matrix: float32 [16384, 16384], P('row', 'col'), as said below
- panel: float32 [16384, 64], P('row'), as said below
Outputs:
- updated: float32 [16384, 16384], P('row', 'col')
- weights: float32 [16384, 64], P('row')
Inputs may be any that keep to these rules, and one draw needn't show every extreme that they name: matrix is exactly symmetric. panel has full column rank.
All inputs are finite; a program needn't handle non-finite values.
Results may differ from a plain program's by a relative error of at most 0.000071.
Values sent between devices are 32-bit elements; how exact they have to be, the bound alone decides.
A program may use at most 64 MiB of HBM per device.

v0:
```python
import jax
import jax.numpy as jnp
from jax import lax
from jax.sharding import PartitionSpec as P


def mul(left, right):
    return jnp.dot(left, right, precision=lax.Precision.HIGHEST, preferred_element_type=jnp.float32)


def local(matrix, panel):
    cols_local = matrix.shape[1]
    col_place = lax.axis_index("col")
    gram = lax.psum(mul(panel.T, panel), "row")
    lower = jnp.linalg.cholesky(gram)
    basis_rows = lax.linalg.triangular_solve(lower, panel.T, left_side=True, lower=True).T
    whole = lax.all_gather(basis_rows, "row", axis=0, tiled=True)
    basis_cols = lax.dynamic_slice_in_dim(whole, col_place * cols_local, cols_local, 0)
    product = lax.psum(mul(matrix, basis_cols), "col")
    coupling = lax.psum(mul(basis_rows.T, product), "row")
    weights_rows = 2.0 * product - 2.0 * mul(basis_rows, coupling)
    whole_weights = lax.all_gather(weights_rows, "row", axis=0, tiled=True)
    weights_cols = lax.dynamic_slice_in_dim(whole_weights, col_place * cols_local, cols_local, 0)
    left_factor = jnp.concatenate([basis_rows, weights_rows], axis=1)
    right_factor = jnp.concatenate([weights_cols, basis_cols], axis=1)
    updated = matrix - mul(left_factor, right_factor.T)
    return (updated, weights_rows)


def solution(mesh):
    in_specs = (P("row", "col"), P("row", None))
    out_specs = (P("row", "col"), P("row", None))
    return jax.shard_map(local, mesh=mesh, in_specs=in_specs, out_specs=out_specs, check_vma=False)
```

profile of v0, /device:TPU:1, one launch (start us, length us, event | category | flops | bytes accessed | tf_op | source)
XLA Modules:
  0.0 604.7 jit_solution(15181882732824194987)
XLA Ops:
  7.2 0.0 copy-start
  7.2 0.0 all-gather.3.cloned.1.call-start
  7.2 0.8 copy-done
  8.1 0.3 fusion.12
  8.3 122.3 %psum.21 = f32[64,64]{0,1:T(8,128)S(1)} all-reduce(f32[64,64]{0,1:T(8,128)S(1)} %fusion.12), channel_id=1, replica_groups=mesh['row'=32,'col'=16] {'row'}, use_global_device_ids=true, to_apply=%region_0.0 | all-reduce | flops 4096 | bytes 32768 | tf_op jit(solution)/shard_map/psum | solution.py:14
  130.7 0.1 copy.5
  130.8 5.8 cholesky.16
  136.6 0.6 compare_reduce_fusion
  137.3 0.7 fusion.7
  137.9 4.9 custom-call.6
  142.8 1.0 fusion.8
  143.8 0.0 copy-start.2
  143.8 0.0 all-gather.3.cloned.1.call-update
  143.9 0.0 all-reduce.2.cloned.1.call-start
  143.9 106.3 %all-gather.3.cloned.1.call-done = f32[16384,64]{0,1:T(8,128)} async-done(((f32[512,64]{0,1:T(8,128)}), f32[16384,64]{0,1:T(8,128)}) %all-gather.3.cloned.1.call-update) | async-done | bytes 4194320 | tf_op jit(solution)/shard_map/all_gather | solution.py:17
  250.2 1.0 constant_dynamic-slice_fusion.1
  251.1 0.0 copy-start.1
  251.2 4.5 convolution_bitcast_fusion
  255.7 0.0 all-reduce.2.cloned.1.call-update
  255.7 0.0 all-gather.5.cloned.1.call-start
  255.7 112.5 %all-reduce.2.cloned.1.call-done = f32[512,64]{0,1:T(8,128)} async-done(((f32[512,64]{0,1:T(8,128)}), f32[512,64]{0,1:T(8,128)}) %all-reduce.2.cloned.1.call-update) | async-done | bytes 131088 | tf_op jit(solution)/shard_map/psum | solution.py:19
  368.2 0.0 copy-done.2
  368.2 1.2 fusion.13
  369.4 115.8 %psum.23 = f32[64,64]{1,0:T(8,128)S(1)} all-reduce(f32[64,64]{1,0:T(8,128)S(1)} %fusion.13), channel_id=1, replica_groups=mesh['row'=32,'col'=16] {'row'}, use_global_device_ids=true, to_apply=%region_4.5 | all-reduce | flops 4096 | bytes 32768 | tf_op jit(solution)/shard_map/psum | solution.py:20
  485.2 1.9 fusion
  487.1 0.0 all-gather.5.cloned.1.call-update
  487.1 106.0 %all-gather.5.cloned.1.call-done = f32[16384,64]{0,1:T(8,128)} async-done(((f32[512,64]{0,1:T(8,128)}), f32[16384,64]{0,1:T(8,128)}) %all-gather.5.cloned.1.call-update) | async-done | bytes 4194320 | tf_op jit(solution)/shard_map/all_gather | solution.py:22
  593.1 1.0 constant_dynamic-slice_fusion
  594.1 0.0 copy-done.1
  594.1 4.1 convolution_subtract_fusion
  (2 shorter events, 0.0 us)
Async XLA Ops:
  7.2 0.9 copy-start
  7.2 243.0 %all-gather.3.cloned.1.call-start = ((), (), s32[]{:S(2)}) async-start(), calls=%async_computation | async-start | bytes 4325376 | tf_op jit(solution)/shard_map/all_gather | solution.py:17
  143.8 224.4 %copy-start.2 = (f32[64,512]{1,0:T(8,128)S(1)}, f32[64,512]{1,0:T(8,128)}, u32[]{:S(2)}) copy-start(f32[64,512]{1,0:T(8,128)} %fusion.8) | copy-start | bytes 393220
  143.9 224.3 %all-reduce.2.cloned.1.call-start = ((), (), s32[]{:S(2)}) async-start(), calls=%async_computation.1 | async-start | bytes 262144 | tf_op jit(solution)/shard_map/psum | solution.py:19
  251.1 342.9 %copy-start.1 = (f32[512,1024]{1,0:T(8,128)S(1)}, f32[512,1024]{1,0:T(8,128)}, u32[]{:S(2)}) copy-start(f32[512,1024]{1,0:T(8,128)} %param.2) | copy-start | bytes 6291460
  255.7 337.4 %all-gather.5.cloned.1.call-start = ((), (), s32[]{:S(2)}) async-start(), calls=%async_computation.2 | async-start | bytes 4325376 | tf_op jit(solution)/shard_map/all_gather | solution.py:22
Sparse Core Ops, SparseCore 0:
  144.0 106.1 all-gather.2
  255.8 112.3 all-reduce.1
  487.2 105.8 all-gather.4
where the time goes:
time: 607 us; the launch traced here: 605 us
  waiting for transfers between devices  325 us (54%)
  blocking collectives  238 us (39%)
  between operations  13.8 us (2%)
  matrix products  12.9 us (2%)
  other arithmetic  12.1 us (2%)
    psum x1, blocking collectives, local(): gram = lax.psum(mul(panel.T, panel), 'row')  122 us
    psum x1, blocking collectives, local(): coupling = lax.psum(mul(basis_rows.T, product), 'row')  116 us
    psum x1, waiting for transfers between devices, local(): product = lax.psum(mul(matrix, basis_cols), 'col')  112 us
    all_gather x1, waiting for transfers between devices, local(): whole = lax.all_gather(basis_rows, 'row', axis=0, tiled=True)  106 us
    all_gather x1, waiting for transfers between devices, local(): whole_weights = lax.all_gather(weights_rows, 'row', axis=0, tiled=True)  106 us
  transfers between devices with their start and end apart: 3, of which 3 were waited for; matrix products, arithmetic and copies ran while one was open for 0% of the time, Pallas kernels for 0%

commit v1 on v0

v1 whole, which is shorter than its diff:
```python
import jax
import jax.numpy as jnp
from jax import lax
from jax.experimental import pallas as pl
from jax.experimental.pallas import tpu as pltpu
from jax.sharding import PartitionSpec as P

MESH = pl.DeviceIdType.MESH
F32 = jnp.float32
BF16 = jnp.bfloat16
NX, NZ, NC = 4, 8, 16
NR = NX * NZ
B = 64
RL, CL = 512, 1024
TINY = 1e-30
G_RS, G_AG, P_PL, P_Y, Z_RS, Y_AG, Y_A, Y_B, S_Y, S_AG = range(10)


def dot(a, b, dims=((1,), (0,))):
    return lax.dot_general(a, b, (dims, ((), ())), precision=lax.Precision.HIGHEST, preferred_element_type=F32)


def split(x):
    high = x.astype(BF16)
    return high, (x - high.astype(F32)).astype(BF16)


def factors(matrix_hbm, panel_hbm, fr_ref, fc_ref, w_ref,
            a_v, p_v, pt, zt, zsend, zrecv, gsend, grecv, gown, gall,
            pown, pplane, pcols, ypiece, yrow2, yall, yline, yrows, srow, stotal, sline, sall,
            ct, yct, yrt, in_sem, send_sem, recv_sem):
    r = lax.axis_index("row")
    c = lax.axis_index("col")
    x, z = r // NZ, r % NZ

    load_p = pltpu.make_async_copy(panel_hbm, p_v, in_sem.at[0])
    load_a = pltpu.make_async_copy(matrix_hbm, a_v, in_sem.at[1])
    load_p.start()
    load_a.start()

    def plane(i):
        return lax.rem(x + i // NZ, NX) * NZ + lax.rem(z + lax.rem(i, NZ), NZ)

    def line(i):
        return lax.rem(c + i, NC)

    barrier = pltpu.get_barrier_semaphore()

    def greet_plane(i, carry):
        pl.semaphore_signal(barrier, inc=1, device_id=(plane(i), c), device_id_type=MESH)
        return carry

    def greet_line(i, carry):
        pl.semaphore_signal(barrier, inc=1, device_id=(r, line(i)), device_id_type=MESH)
        return carry

    lax.fori_loop(1, NR, greet_plane, 0)
    lax.fori_loop(1, NC, greet_line, 0)

    def to_plane(stage, src, dst):
        def send(i, carry):
            other = plane(i)
            pltpu.make_async_remote_copy(
                src(other), dst, send_sem.at[stage], recv_sem.at[stage],
                device_id=(other, c), device_id_type=MESH).start()
            return carry
        lax.fori_loop(1, NR, send, 0)

    def to_line(stage, src, dst):
        def send(i, carry):
            other = line(i)
            pltpu.make_async_remote_copy(
                src(other), dst, send_sem.at[stage], recv_sem.at[stage],
                device_id=(r, other), device_id_type=MESH).start()
            return carry
        lax.fori_loop(1, NC, send, 0)

    def arrived(stage, buf, n):
        part = buf.at[pl.ds(0, n)]
        pltpu.make_async_copy(part, part, recv_sem.at[stage]).wait()

    def left(stage, buf, n):
        part = buf.at[pl.ds(0, n)]
        pltpu.make_async_copy(part, part, send_sem.at[stage]).wait()

    load_p.wait()
    pt[...] = p_v[...].T
    own_scale = jnp.maximum(jnp.max(jnp.abs(pt[...]), axis=1, keepdims=True), TINY)
    gram = dot(pt[...], pt[...], ((1,), (1,)))
    scale_wide = jnp.broadcast_to(own_scale, (B, 128))
    gsend[:, 0, :] = jnp.concatenate([gram[:32], gram[32:]], axis=1)
    gsend[:, 1, :] = scale_wide[:32]
    gsend[:, 2, :] = scale_wide[32:]
    gsend[:, 3, :] = scale_wide[32:]
    for q in range(4):
        for g in range(4):
            pown[:, q * 4 + g, :] = pt[pl.ds(16 * q, 16), pl.ds(128 * g, 128)]

    pscaled = pt[...] * (1.0 / (128.0 * own_scale))
    load_a.wait()
    zt[...] = dot(pscaled, a_v[...])
    for h in range(2):
        for p in range(2):
            for g in range(4):
                zsend[:, h * 8 + p * 4 + g, :] = zt[pl.ds(32 * p, 32), pl.ds(512 * h + 128 * g, 128)]

    pl.semaphore_wait(barrier, NR - 1 + NC - 1)

    to_plane(G_RS, lambda o: gsend.at[o], grecv.at[r])
    to_plane(Z_RS, lambda o: zsend.at[o], zrecv.at[r])
    to_plane(P_PL, lambda o: pown.at[c], pplane.at[r])
    grecv[r] = gsend[r]
    zrecv[r] = zsend[r]
    pplane[r] = pown[c]

    arrived(G_RS, grecv, NR - 1)
    gown[0, :] = jnp.sum(grecv[:, 0, :], axis=0)
    top = jnp.max(grecv[:, 1:3, :], axis=0)
    gown[1:3, :] = top
    gown[3, :] = top[1]
    to_plane(G_AG, lambda o: gown, gall.at[r])
    gall[r] = gown[...]

    arrived(P_PL, pplane, NR - 1)
    to_line(P_Y, lambda o: pplane.at[pl.ds(2 * o, 2)], pcols.at[c])
    pcols[c] = pplane[pl.ds(2 * c, 2)]

    arrived(Z_RS, zrecv, NR - 1)
    share = grecv[:, 1:3, :] / top[None]
    for h in range(2):
        for p in range(2):
            rows = pl.ds(h * 8 + p * 4, 4)
            ypiece[rows, :] = jnp.sum(zrecv[:, rows, :] * share[:, p:p + 1, :], axis=0)
    to_plane(Y_AG, lambda o: ypiece, yall.at[r])
    to_line(Y_A, lambda o: ypiece, yline.at[c])
    yall[r] = ypiece[...]
    yline[c] = ypiece[...]
    yrow2[...] = jnp.zeros_like(yrow2)
    for h in range(2):
        for p in range(2):
            for g in range(4):
                yrow2[pl.ds(p, 1), pl.ds(512 * h + 128 * g, 128)] = ypiece[pl.ds(h * 8 + p * 4 + g, 1), :]

    arrived(G_AG, gall, NR - 1)
    scale = jnp.concatenate([gall[:, 1, :], gall[:, 2, :]], axis=0) * 128.0
    inv_scale = 1.0 / scale

    arrived(P_Y, pcols, NC - 1)
    for h in range(2):
        for q in range(4):
            for g in range(4):
                block = pcols[:, h, q * 4 + g, :]
                ct[pl.ds(16 * q, 16), pl.ds(512 * h + 128 * g, 128)] = block * inv_scale[16 * q:16 * q + 16]
    part = dot(yrow2[...], ct[...], ((1,), (1,)))
    srow[...] = jnp.concatenate([part[0:1], part[1:2]], axis=1)
    to_line(S_Y, lambda o: srow, sline.at[c])
    sline[c] = srow[...]

    arrived(Y_A, yline, NC - 1)

    def send_rows(i, carry):
        other = plane(i)
        pltpu.make_async_remote_copy(
            yline.at[other // 2, pl.ds(pl.multiple_of(lax.rem(other, 2) * 8, 8), 8)], yrows.at[r],
            send_sem.at[Y_B], recv_sem.at[Y_B],
            device_id=(other, c), device_id_type=MESH).start()
        return carry
    lax.fori_loop(1, NR, send_rows, 0)
    yrows[r] = yline[r // 2, pl.ds(pl.multiple_of(lax.rem(r, 2) * 8, 8), 8), :]

    g32 = gall[:, 0, :]
    gram = jnp.concatenate([g32[:, :B], g32[:, B:]], axis=0)
    inv64 = inv_scale[:, :B]
    gram = gram * inv64 * inv64.T
    row_id = lax.broadcasted_iota(jnp.int32, (B, 2 * B), 0)
    lane_id = lax.broadcasted_iota(jnp.int32, (B, 2 * B), 1)
    work = jnp.concatenate([gram, jnp.where(row_id == lane_id, 1.0, 0.0)[:, :B]], axis=1)
    for j in range(B - 1):
        ratio = work[:, j:j + 1] * (1.0 / work[j:j + 1, j:j + 1])
        work = work - jnp.where(row_id > j, ratio, 0.0) * work[j:j + 1, :]
    pivots = jnp.sum(jnp.where(row_id == lane_id, work, 0.0), axis=1, keepdims=True)
    root = lax.rsqrt(pivots)
    root = root * (1.5 - 0.5 * pivots * root * root)
    inv_lower = work[:, B:] * root

    arrived(S_Y, sline, NC - 1)
    stotal[...] = jnp.sum(sline[...], axis=0)
    to_plane(S_AG, lambda o: stotal, sall.at[r])
    sall[r] = stotal[...]

    basis_r = dot(inv_lower, pt[...] * inv_scale[:, :1])
    basis_c = dot(inv_lower, ct[...])

    arrived(Y_AG, yall, NR - 1)
    for h in range(2):
        for p in range(2):
            for g in range(4):
                yct[pl.ds(32 * p, 32), pl.ds(512 * h + 128 * g, 128)] = yall[:, h * 8 + p * 4 + g, :]
    product_c = dot(inv_lower, yct[...])
    arrived(Y_B, yrows, NR - 1)
    for p in range(2):
        for g in range(4):
            yrt[pl.ds(32 * p, 32), pl.ds(128 * g, 128)] = yrows[:, p * 4 + g, :]
    product_r = dot(inv_lower, yrt[...])

    arrived(S_AG, sall, NR - 1)
    s32 = sall[:, 0, :]
    inner = jnp.concatenate([s32[:, :B], s32[:, B:]], axis=0)
    coupling = dot(dot(inv_lower, inner), inv_lower, ((1,), (1,)))
    weights_r = 2.0 * product_r - 2.0 * dot(coupling, basis_r)
    weights_c = 2.0 * product_c - 2.0 * dot(coupling, basis_c)

    left_t = jnp.concatenate([basis_r, weights_r], axis=0).T
    w_ref[...] = left_t[:, B:]
    high, low = split(left_t)
    fr_ref[:, 0:128] = high
    fr_ref[:, 128:256] = low
    fr_ref[:, 256:384] = high
    high, low = split(jnp.concatenate([weights_c, basis_c], axis=0))
    fc_ref[0:128, :] = high
    fc_ref[128:256, :] = high
    fc_ref[256:384, :] = low

    left(G_RS, gsend, NR - 1)
    left(G_AG, gall, NR - 1)
    left(P_PL, pplane, NR - 1)
    left(P_Y, pcols, NC - 1)
    left(Z_RS, zsend, NR - 1)
    left(Y_AG, yall, NR - 1)
    left(Y_A, yline, NC - 1)
    left(Y_B, yrows, NR - 1)
    left(S_Y, sline, NC - 1)
    left(S_AG, sall, NR - 1)


def apply_update(matrix_ref, fr_ref, fc_ref, w_ref, out_ref, w_out):
    out_ref[...] = matrix_ref[...] - jnp.dot(fr_ref[...], fc_ref[...], preferred_element_type=F32)

    @pl.when(pl.program_id(0) == 0)
    def _():
        w_out[...] = w_ref[...]


def local(matrix, panel):
    vmem = pl.BlockSpec(memory_space=pltpu.VMEM)
    anywhere = pl.BlockSpec(memory_space=pl.ANY)
    fr, fc, w = pl.pallas_call(
        factors,
        out_shape=(jax.ShapeDtypeStruct((RL, 384), BF16), jax.ShapeDtypeStruct((384, CL), BF16),
                   jax.ShapeDtypeStruct((RL, B), F32)),
        in_specs=[anywhere, anywhere],
        out_specs=(vmem, vmem, vmem),
        scratch_shapes=[
            pltpu.VMEM((RL, CL), F32), pltpu.VMEM((RL, B), F32), pltpu.VMEM((B, RL), F32),
            pltpu.VMEM((B, CL), F32),
            pltpu.VMEM((NR, 16, 128), F32), pltpu.VMEM((NR, 16, 128), F32),
            pltpu.VMEM((NR, 4, 128), F32), pltpu.VMEM((NR, 4, 128), F32),
            pltpu.VMEM((4, 128), F32), pltpu.VMEM((NR, 4, 128), F32),
            pltpu.VMEM((NC, 16, 128), F32), pltpu.VMEM((NR, 16, 128), F32), pltpu.VMEM((NC, 2, 16, 128), F32),
            pltpu.VMEM((16, 128), F32), pltpu.VMEM((8, CL), F32), pltpu.VMEM((NR, 16, 128), F32),
            pltpu.VMEM((NC, 16, 128), F32), pltpu.VMEM((NR, 8, 128), F32),
            pltpu.VMEM((1, 128), F32), pltpu.VMEM((1, 128), F32),
            pltpu.VMEM((NC, 1, 128), F32), pltpu.VMEM((NR, 1, 128), F32),
            pltpu.VMEM((B, CL), F32), pltpu.VMEM((B, CL), F32), pltpu.VMEM((B, RL), F32),
            pltpu.SemaphoreType.DMA((2,)), pltpu.SemaphoreType.DMA((10,)), pltpu.SemaphoreType.DMA((10,)),
        ],
        compiler_params=pltpu.CompilerParams(
            collective_id=0, has_side_effects=True, vmem_limit_bytes=40 << 20),
        name="factors",
    )(matrix, panel)
    tile = 128
    return pl.pallas_call(
        apply_update,
        grid=(RL // tile,),
        out_shape=(jax.ShapeDtypeStruct((RL, CL), F32), jax.ShapeDtypeStruct((RL, B), F32)),
        in_specs=[pl.BlockSpec((tile, CL), lambda i: (i, 0)), pl.BlockSpec((tile, 384), lambda i: (i, 0)),
                  pl.BlockSpec((384, CL), lambda i: (0, 0)), pl.BlockSpec((RL, B), lambda i: (0, 0))],
        out_specs=(pl.BlockSpec((tile, CL), lambda i: (i, 0)), pl.BlockSpec((RL, B), lambda i: (0, 0))),
        name="apply_update",
    )(matrix, fr, fc, w)


def solution(mesh):
    specs = (P("row", "col"), P("row", None))
    return jax.shard_map(local, mesh=mesh, in_specs=specs, out_specs=specs, check_vma=False)
```

time: 607 us -> 69.4 us (0.11)
  waiting for transfers between devices: 325 us -> 0 us
  blocking collectives: 238 us -> 0 us
  Pallas kernels: 0 us -> 61.8 us
  between operations: 13.8 us -> 0.66 us
  matrix products: 12.9 us -> 0 us
  other arithmetic: 12.1 us -> 0 us
    psum x2 -> x0, blocking collectives: 238 us -> none  [the longest x1 122 us: local(): gram = lax.psum(mul(panel.T, panel), 'row')]
    all_gather x2 -> x0, waiting for transfers between devices: 212 us -> none  [the longest x1 106 us: local(): whole = lax.all_gather(basis_rows, 'row', axis=0, tiled=True)]
    psum x1 -> x0, waiting for transfers between devices: 112 us -> none  [local(): product = lax.psum(mul(matrix, basis_cols), 'col')]
    pallas_call x0 -> x2, Pallas kernels: none -> 61.8 us  [the longest x1 57 us: local(): pl.pallas_call(factors, out_shape=(jax.ShapeDtypeStruct((RL, 384), BF16),...]
    another operation x5 -> x0, other arithmetic: 12.1 us -> none  [the longest x3 6.52 us: local(): lower = jnp.linalg.cholesky(gram)]
    dot_general x5 -> x0, matrix products: 11.9 us -> none  [mul(): jnp.dot(left, right, precision=lax.Precision.HIGHEST, preferred_element_t...]
  transfers between devices with their start and end apart: 3 -> 0, of which waited for: 3 -> 0; matrix products, arithmetic and copies ran while one was open for 0% -> 0% of each run, Pallas kernels for 0% -> 0%
where the time goes in v1:
time: 69.4 us; the launch traced here: 69.2 us
  Pallas kernels  61.8 us (89%)
  local copies, waits for them, and re-layouts  6.69 us (10%)
    pallas_call x1, Pallas kernels, local(): pl.pallas_call(factors, out_shape=(jax.ShapeDtypeStruct((RL, 384), BF16),...  57 us
    unnamed x9, local copies, waits for them, and re-layouts  4.97 us
    pallas_call x1, Pallas kernels, local(): pl.pallas_call(apply_update, grid=(RL // tile,), out_shape=(jax.ShapeDtyp...  4.76 us
    pallas_call x1, local copies, waits for them, and re-layouts, local(): pl.pallas_call(apply_update, grid=(RL // tile,), out_shape=(jax.ShapeDtyp...  1.72 us

profile of v1, /device:TPU:1, one launch (start us, length us, event | category | flops | bytes accessed | tf_op | source)
XLA Modules:
  0.0 69.2 jit_solution(11233574526655092402)
XLA Ops:
  0.6 1.0 %copy.4.panel_hbm = f32[512,64]{1,0:T(8,128)S(1)} copy(f32[512,64]{0,1:T(8,128)} %param.3) | data formatting | bytes 262144 | tf_op args[1]
  1.7 0.0 copy-start
  1.7 1.6 %copy-done = f32[512,1024]{1,0:T(8,128)S(1)} copy-done((f32[512,1024]{1,0:T(8,128)S(1)}, f32[512,1024]{1,0:T(8,128)}, u32[]{:S(2)}) %copy-start) | copy-done | bytes 2097176
  3.3 57.0 %factors.1 = (bf16[512,384]{1,0:T(8,128)(2,1)S(1)}, bf16[384,1024]{1,0:T(8,128)(2,1)S(1)}, f32[512,64]{1,0:T(8,128)S(1)}) custom-call(f32[512,1024]{1,0:T(8,128)S(1)} %copy-done, f32[512,64]{1,0:T(8,128)S(1)} %copy.4.panel_hbm), custom_call_target="tpu_custom_call" | custom-call | tf_op jit(solution)/shard_map/factors/pallas_call | solution.py:247
  60.3 0.0 copy-start.1
  60.3 0.9 %copy-done.1 = bf16[384,1024]{1,0:T(8,128)(2,1)} copy-done((bf16[384,1024]{1,0:T(8,128)(2,1)}, bf16[384,1024]{1,0:T(8,128)(2,1)S(1)}, u32[]{:S(2)}) %copy-start.1) | copy-done | bytes 786456
  61.2 0.0 copy-start.2
  61.2 0.7 %copy-done.2 = bf16[512,384]{1,0:T(8,128)(2,1)} copy-done((bf16[512,384]{1,0:T(8,128)(2,1)}, bf16[512,384]{1,0:T(8,128)(2,1)S(1)}, u32[]{:S(2)}) %copy-start.2) | copy-done | bytes 393240
  62.0 0.0 copy-start.3
  62.0 0.7 %copy-done.3 = f32[512,64]{1,0:T(8,128)} copy-done((f32[512,64]{1,0:T(8,128)}, f32[512,64]{1,0:T(8,128)S(1)}, u32[]{:S(2)}) %copy-start.3) | copy-done | bytes 131096
  62.7 4.8 %apply_update.1 = (f32[512,1024]{1,0:T(8,128)}, f32[512,64]{1,0:T(8,128)}) custom-call(f32[512,1024]{1,0:T(8,128)} %matrix_ref.1, bf16[512,384]{1,0:T(8,128)(2,1)} %copy-done.2, bf16[384,1024]{1,0:T(8,128)(2,1)} %copy-done.1, f32[512,64]{1,0:T(8,128)} %copy-done.3), custom_call_target="tpu_custom_call" | custom-call | tf_op jit(solution)/shard_map/apply_update/pallas_call | solution.py:272
  67.4 1.7 %copy.5 = f32[512,64]{0,1:T(8,128)} copy(f32[512,64]{1,0:T(8,128)} %get-tuple-element.9) | data formatting | bytes 262144 | tf_op jit(solution)/shard_map/apply_update/pallas_call | solution.py:272
Async XLA Ops:
  1.7 1.6 %copy-start = (f32[512,1024]{1,0:T(8,128)S(1)}, f32[512,1024]{1,0:T(8,128)}, u32[]{:S(2)}) copy-start(f32[512,1024]{1,0:T(8,128)} %matrix_ref.1) | copy-start | bytes 6291460
  60.3 0.9 %copy-start.1 = (bf16[384,1024]{1,0:T(8,128)(2,1)}, bf16[384,1024]{1,0:T(8,128)(2,1)S(1)}, u32[]{:S(2)}) copy-start(bf16[384,1024]{1,0:T(8,128)(2,1)S(1)} %get-tuple-element.6.fc_ref) | copy-start | bytes 2359300
  61.2 0.8 %copy-start.2 = (bf16[512,384]{1,0:T(8,128)(2,1)}, bf16[512,384]{1,0:T(8,128)(2,1)S(1)}, u32[]{:S(2)}) copy-start(bf16[512,384]{1,0:T(8,128)(2,1)S(1)} %get-tuple-element.5.fr_ref) | copy-start | bytes 1179652
  62.0 0.7 %copy-start.3 = (f32[512,64]{1,0:T(8,128)}, f32[512,64]{1,0:T(8,128)S(1)}, u32[]{:S(2)}) copy-start(f32[512,64]{1,0:T(8,128)S(1)} %get-tuple-element.7.w_ref) | copy-start | bytes 393220

commit v2 on v0

v2 whole, which is shorter than its diff:
```python
import jax
import jax.numpy as jnp
from jax import lax
from jax.experimental import pallas as pl
from jax.experimental.pallas import tpu as pltpu
from jax.sharding import PartitionSpec as P

MESH = pl.DeviceIdType.MESH
F32 = jnp.float32
BF16 = jnp.bfloat16
NX, NZ, NC = 4, 8, 16
NR = NX * NZ
NG = NX * NC
B = 64
RL, CL = 512, 1024
QL = 256
TINY = 1e-30
G_RS, G_AG, P_SUB, P_ZR, P_XR, Z_RS, Y_AG, Y_B, S_RS, S_AG = range(10)
STAGES = 10


def dot(a, b, dims=((1,), (0,))):
    return lax.dot_general(a, b, (dims, ((), ())), precision=lax.Precision.HIGHEST, preferred_element_type=F32)


def split(x):
    high = x.astype(BF16)
    return high, (x - high.astype(F32)).astype(BF16)


def split3(x):
    high = x.astype(BF16)
    rest = x - high.astype(F32)
    mid = rest.astype(BF16)
    return high, mid, (rest - mid.astype(F32)).astype(BF16)


def dot6(a, b):
    parts = jnp.concatenate(split3(a), axis=0)
    bh, bm, bl = split3(b)
    one = jnp.dot(parts, bh, preferred_element_type=F32)
    two = jnp.dot(parts[:2 * B], bm, preferred_element_type=F32)
    three = jnp.dot(parts[:B], bl, preferred_element_type=F32)
    return one[:B] + ((one[B:2 * B] + two[:B]) + (one[2 * B:] + two[B:] + three))


def dot3(at, b):
    ah, al = split(at.T)
    bh, bl = split(b)
    return jnp.dot(jnp.concatenate([ah, al, ah], axis=1), jnp.concatenate([bh, bh, bl], axis=0),
                   preferred_element_type=F32)


def inverse_factor(gram):
    row_id = lax.broadcasted_iota(jnp.int32, (B, 2 * B), 0)
    lane_id = lax.broadcasted_iota(jnp.int32, (B, 2 * B), 1)
    work = jnp.concatenate([gram, jnp.where(row_id == lane_id, 1.0, 0.0)[:, :B]], axis=1)
    step = 8
    for j in range(0, B, step):
        cols = [jnp.broadcast_to(work[:, j + t:j + t + 1], (B, 2 * B)) for t in range(step)]
        rows = [work[j + t:j + t + 1, :] for t in range(step)]
        for t in range(step):
            at = j + t
            ratio = jnp.where(row_id > at, cols[t] * (1.0 / cols[t][at:at + 1, :]), 0.0)
            work = work - ratio * rows[t]
            for u in range(t + 1, step):
                cols[u] = cols[u] - ratio * cols[t][j + u:j + u + 1, :]
                rows[u] = rows[u] - ratio[j + u:j + u + 1, :] * rows[t]
    pivots = jnp.sum(jnp.where(row_id == lane_id, work, 0.0), axis=1, keepdims=True)
    root = lax.rsqrt(pivots)
    root = root * (1.5 - 0.5 * pivots * root * root)
    return work[:, B:] * root


def panel_step(matrix_hbm, panel_hbm, out_ref, w_ref,
               pt, zt, zrecv, gsend, grecv, gown, gall, ct, spart,
               ypiece, yct, yrt, ssend, srecv, sown, sall, in_sem, send_sem, recv_sem):
    r = lax.axis_index("row")
    c = lax.axis_index("col")
    x, z = r // NZ, r % NZ
    feats = pl.ds(pl.multiple_of(z * 8, 8), 8)
    quarter = pl.ds(pl.multiple_of(x * QL, QL), QL)
    half = pl.ds(pl.multiple_of(lax.rem(x, 2) * QL, QL), QL)

    load_p = pltpu.make_async_copy(panel_hbm, pt, in_sem.at[0])
    load_a = pltpu.make_async_copy(matrix_hbm, out_ref, in_sem.at[1])
    load_p.start()
    load_a.start()

    def plane(i):
        return lax.rem(x + i // NZ, NX) * NZ + lax.rem(z + lax.rem(i, NZ), NZ)

    def line(i):
        return lax.rem(c + i, NC)

    barrier = pltpu.get_barrier_semaphore()

    def greet_plane(i, carry):
        pl.semaphore_signal(barrier, inc=1, device_id=(plane(i), c), device_id_type=MESH)
        return carry

    def greet_line(i, carry):
        pl.semaphore_signal(barrier, inc=1, device_id=(r, line(i)), device_id_type=MESH)
        return carry

    lax.fori_loop(1, NR, greet_plane, 0)
    lax.fori_loop(1, NC, greet_line, 0)

    def push(stage, src, dst, row, col):
        pltpu.make_async_remote_copy(
            src, dst, send_sem.at[stage], recv_sem.at[stage],
            device_id=(row, col), device_id_type=MESH).start()

    def to_plane(stage, src, dst):
        def send(i, carry):
            other = plane(i)
            push(stage, src(other), dst, other, c)
            return carry
        lax.fori_loop(1, NR, send, 0)

    def to_line(stage, src, dst):
        def send(i, carry):
            other = line(i)
            push(stage, src(other), dst, r, other)
            return carry
        lax.fori_loop(1, NC, send, 0)

    def arrived(stage, part):
        pltpu.make_async_copy(part, part, recv_sem.at[stage]).wait()

    def left(stage, part):
        pltpu.make_async_copy(part, part, send_sem.at[stage]).wait()

    def first(buf, n):
        return buf.at[pl.ds(0, n)]

    load_p.wait()
    own_scale = jnp.maximum(jnp.max(jnp.abs(pt[...]), axis=1, keepdims=True), TINY)
    gram = dot(pt[...], pt[...], ((1,), (1,)))
    gsend[:, 0, :] = jnp.concatenate([gram[:32], gram[32:]], axis=1)
    scale_row = jnp.broadcast_to(own_scale, (B, 128)).T[0:1, :]
    gsend[:, 1, :] = jnp.broadcast_to(jnp.concatenate([scale_row, scale_row], axis=1), (NR, 128))

    def multiply():
        load_a.wait()
        zt[...] = dot6(pt[...] * (1.0 / (128.0 * own_scale)), out_ref[...])

    @pl.when(z < NZ // 2)
    def _():
        multiply()

    pl.semaphore_wait(barrier, NR - 1 + NC - 1)
    def spread_quarters(i, carry):
        ox = 2 * lax.rem(r, 2) + i // NZ
        oz = lax.rem(z + lax.rem(i, NZ), NZ)
        other = ox * NZ + oz

        @pl.when(other != r)
        def _():
            push(P_SUB, pt.at[pl.ds(pl.multiple_of(oz * 8, 8), 8), pl.ds(pl.multiple_of((i // NZ) * QL, QL), QL)],
                 ct.at[pl.ds(pl.multiple_of(oz * 8, 8), 8), pl.ds(pl.multiple_of(ox * QL, QL), QL)], other, c)
        return carry

    @pl.when(c == r // 2)
    def _():
        lax.fori_loop(0, 2 * NZ, spread_quarters, 0)

    own_quarter = r == 2 * c + x // 2

    @pl.when(own_quarter)
    def _():
        ct[feats, quarter] = pt[feats, half]

    to_plane(G_RS, lambda o: gsend.at[o], grecv.at[r])
    grecv[r] = gsend[r]

    @pl.when(z >= NZ // 2)
    def _():
        multiply()

    def send_pieces(i, carry):
        other = plane(i)
        push(Z_RS, zt.at[pl.ds(pl.multiple_of(lax.rem(other, NZ) * 8, 8), 8),
                         pl.ds(pl.multiple_of((other // NZ) * QL, QL), QL)], zrecv.at[r], other, c)
        return carry
    lax.fori_loop(1, NR, send_pieces, 0)
    zrecv[r] = zt[feats, quarter]

    @pl.when(jnp.logical_not(own_quarter))
    def _():
        arrived(P_SUB, ct.at[feats, quarter])

    def hand_round(i, carry):
        push(P_ZR, ct.at[feats, quarter], ct.at[feats, quarter], x * NZ + lax.rem(z + i, NZ), c)
        return carry
    lax.fori_loop(1, NZ, hand_round, 0)

    arrived(G_RS, first(grecv, NR - 1))
    gown[...] = jnp.sum(grecv[:, 0, :], axis=0, keepdims=True)
    to_plane(G_AG, lambda o: gown, gall.at[r])
    gall[r] = gown[...]
    scales = jnp.broadcast_to(grecv[:, 1, :][None], (4, NR, 128)).reshape(4 * NR, 128).T[:B]
    scale = jnp.max(scales, axis=1, keepdims=True)
    inv_scale = 1.0 / (128.0 * scale)
    spart[...] = scales * (1.0 / scale)
    share = spart[feats, :]

    arrived(P_ZR, first(zrecv, NZ - 1))
    arrived(Z_RS, first(zrecv, NR - 1))
    total = zrecv[0] * share[:, 0:1]
    for k in range(1, NR):
        total = total + zrecv[k] * share[:, k:k + 1]
    ypiece[...] = total
    part = dot(total, ct[:, quarter] * inv_scale, ((1,), (1,)))
    ssend[...] = jnp.concatenate([part[:4], part[4:]], axis=1)

    def send_coupling(i, carry):
        push(S_RS, ssend, srecv.at[x * NC + c],
             lax.rem(x + i // NC, NX) * NZ + z, lax.rem(c + lax.rem(i, NC), NC))
        return carry
    lax.fori_loop(1, NG, send_coupling, 0)
    srecv[x * NC + c] = ssend[...]

    def send_rows(i, carry):
        block = 2 * c + x // 2
        other = line(i)

        @pl.when(jnp.logical_or(block != r, other != c))
        def _():
            push(Y_B, ypiece, yrt.at[feats, half], block, other)
        return carry
    lax.fori_loop(0, NC, send_rows, 0)

    @pl.when(own_quarter)
    def _():
        yrt[feats, half] = total
    to_plane(Y_AG, lambda o: ypiece, yct.at[feats, quarter])
    yct[feats, quarter] = total

    def hand_across(i, carry):
        push(P_XR, ct.at[:, quarter], ct.at[:, quarter], lax.rem(x + i, NX) * NZ + z, c)
        return carry
    lax.fori_loop(1, NX, hand_across, 0)

    arrived(G_AG, first(gall, NR - 1))
    g32 = gall[:, 0, :]
    gram = jnp.concatenate([g32[:, :B], g32[:, B:]], axis=0)
    inv_row = jnp.broadcast_to(inv_scale, (B, 128)).T[0:1, :]
    inv_lower = inverse_factor(gram * inv_scale * inv_row)
    unscaled = inv_lower * inv_row
    basis_r = dot(unscaled, pt[...])

    arrived(S_RS, first(srecv, NG - 1))
    sown[...] = jnp.sum(srecv[...], axis=0)

    def send_rows_of_coupling(i, carry):
        push(S_AG, sown, sall.at[z], x * NZ + lax.rem(z + i, NZ), c)
        return carry
    lax.fori_loop(1, NZ, send_rows_of_coupling, 0)
    sall[z] = sown[...]

    arrived(Y_AG, first(zrecv, NR - 1))
    product_c = dot(inv_lower, yct[...])

    arrived(P_XR, ct.at[:, pl.ds(0, (NX - 1) * QL)])
    basis_c = dot(unscaled, ct[...])

    @pl.when(own_quarter)
    def _():
        arrived(Y_B, first(zrecv, 15))

    @pl.when(jnp.logical_not(own_quarter))
    def _():
        arrived(Y_B, first(zrecv, 16))
    product_r = dot(inv_lower, yrt[...])

    tile = 128
    for t in range(RL // tile):
        cols = pl.ds(t * tile, tile)
        ours = jnp.concatenate([basis_r[:, t * tile:(t + 1) * tile], product_r[:, t * tile:(t + 1) * tile]], axis=0)
        out_ref[cols, :] -= dot3(2.0 * ours, jnp.concatenate([product_c, basis_c], axis=0))

    arrived(S_AG, first(sall, NZ - 1))
    inner = jnp.concatenate([sall[k][:, h * B:(h + 1) * B] for k in range(NZ) for h in range(2)], axis=0)
    coupling = dot(dot(inv_lower, inner), inv_lower, ((1,), (1,)))
    w_ref[...] = 2.0 * product_r - 2.0 * dot(coupling, basis_r)
    turned = 4.0 * dot(coupling, basis_c)
    for t in range(RL // tile):
        cols = pl.ds(t * tile, tile)
        out_ref[cols, :] += dot3(basis_r[:, t * tile:(t + 1) * tile], turned)

    left(G_RS, first(gsend, NR - 1))
    left(G_AG, first(gall, NR - 1))
    left(Z_RS, first(zrecv, NR - 1))
    left(P_XR, ct.at[:, pl.ds(0, (NX - 1) * QL)])
    left(Y_AG, first(zrecv, NR - 1))
    left(P_ZR, first(zrecv, NZ - 1))
    left(S_RS, first(srecv, NG - 1))
    left(S_AG, first(sall, NZ - 1))

    @pl.when(own_quarter)
    def _():
        left(Y_B, first(zrecv, 15))

    @pl.when(jnp.logical_not(own_quarter))
    def _():
        left(Y_B, first(zrecv, 16))

    @pl.when(own_quarter)
    def _():
        left(P_SUB, first(zrecv, 15))

    @pl.when(jnp.logical_and(c == r // 2, jnp.logical_not(own_quarter)))
    def _():
        left(P_SUB, first(zrecv, 16))


def local(matrix, panel):
    vmem = pl.BlockSpec(memory_space=pltpu.VMEM)
    in_hbm = pl.BlockSpec(memory_space=pltpu.HBM)
    updated, weights = pl.pallas_call(
        panel_step,
        out_shape=(jax.ShapeDtypeStruct((RL, CL), F32), jax.ShapeDtypeStruct((B, RL), F32)),
        in_specs=[in_hbm, in_hbm],
        out_specs=(vmem, vmem),
        scratch_shapes=[
            pltpu.VMEM((B, RL), F32),
            pltpu.VMEM((B, CL), F32),
            pltpu.VMEM((NR, 8, QL), F32),
            pltpu.VMEM((NR, 2, 128), F32),
            pltpu.VMEM((NR, 2, 128), F32),
            pltpu.VMEM((1, 128), F32),
            pltpu.VMEM((NR, 1, 128), F32),
            pltpu.VMEM((B, CL), F32),
            pltpu.VMEM((B, 128), F32),
            pltpu.VMEM((8, QL), F32),
            pltpu.VMEM((B, CL), F32),
            pltpu.VMEM((B, RL), F32),
            pltpu.VMEM((4, 128), F32),
            pltpu.VMEM((NG, 4, 128), F32),
            pltpu.VMEM((4, 128), F32),
            pltpu.VMEM((NZ, 4, 128), F32),
            pltpu.SemaphoreType.DMA((2,)), pltpu.SemaphoreType.DMA((STAGES,)), pltpu.SemaphoreType.DMA((STAGES,)),
        ],
        compiler_params=pltpu.CompilerParams(
            collective_id=0, has_side_effects=True, vmem_limit_bytes=24 << 20),
        name="panel_step",
    )(pltpu.with_memory_space_constraint(matrix, pltpu.HBM), pltpu.with_memory_space_constraint(panel.T, pltpu.HBM))
    return updated, weights.T


def solution(mesh):
    specs = (P("row", "col"), P("row", None))
    return jax.shard_map(local, mesh=mesh, in_specs=specs, out_specs=specs, check_vma=False)
```

time: 607 us -> 47.2 us (0.08)
  waiting for transfers between devices: 325 us -> 0 us
  blocking collectives: 238 us -> 0 us
  Pallas kernels: 0 us -> 44.4 us
  between operations: 13.8 us -> 0.64 us
  matrix products: 12.9 us -> 0 us
  other arithmetic: 12.1 us -> 0 us
    psum x2 -> x0, blocking collectives: 238 us -> none  [the longest x1 122 us: local(): gram = lax.psum(mul(panel.T, panel), 'row')]
    all_gather x2 -> x0, waiting for transfers between devices: 212 us -> none  [the longest x1 106 us: local(): whole = lax.all_gather(basis_rows, 'row', axis=0, tiled=True)]
    psum x1 -> x0, waiting for transfers between devices: 112 us -> none  [local(): product = lax.psum(mul(matrix, basis_cols), 'col')]
    pallas_call x0 -> x1, Pallas kernels: none -> 44.4 us  [local(): pl.pallas_call(panel_step, out_shape=(jax.ShapeDtypeStruct((RL, CL), F32)...]
    another operation x5 -> x0, other arithmetic: 12.1 us -> none  [the longest x3 6.52 us: local(): lower = jnp.linalg.cholesky(gram)]
    dot_general x5 -> x0, matrix products: 11.9 us -> none  [mul(): jnp.dot(left, right, precision=lax.Precision.HIGHEST, preferred_element_t...]
  transfers between devices with their start and end apart: 3 -> 0, of which waited for: 3 -> 0; matrix products, arithmetic and copies ran while one was open for 0% -> 0% of each run, Pallas kernels for 0% -> 0%
where the time goes in v2:
time: 47.2 us; the launch traced here: 47 us
  Pallas kernels  44.4 us (94%)
  local copies, waits for them, and re-layouts  1.98 us (4%)
  between operations  0.64 us (1%)
    pallas_call x1, Pallas kernels, local(): pl.pallas_call(panel_step, out_shape=(jax.ShapeDtypeStruct((RL, CL), F32)...  44.4 us
    unnamed x2, local copies, waits for them, and re-layouts  1.98 us

profile of v2, /device:TPU:1, one launch (start us, length us, event | category | flops | bytes accessed | tf_op | source)
XLA Modules:
  0.0 47.0 jit_solution(12793765081695771048)
XLA Ops:
  0.6 44.4 %panel_step.1 = (f32[512,1024]{1,0:T(8,128)S(1)}, f32[64,512]{1,0:T(8,128)S(1)}) custom-call(f32[512,1024]{1,0:T(8,128)} %matrix_hbm.1, f32[64,512]{1,0:T(8,128)} %bitcast.3), custom_call_target="tpu_custom_call" | custom-call | tf_op jit(solution)/shard_map/panel_step/pallas_call | solution.py:321
  45.1 1.3 %copy.6 = f32[512,1024]{1,0:T(8,128)} copy(f32[512,1024]{1,0:T(8,128)S(1)} %get-tuple-element.8) | data formatting | bytes 4194304
  46.4 0.7 %copy.7 = f32[512,64]{0,1:T(8,128)} copy(f32[512,64]{0,1:T(8,128)S(1)} %bitcast.2) | data formatting | bytes 262144

commit v3 on v2

--- a/solution.py
+++ b/solution.py
@@ -15,8 +15,8 @@
 RL, CL = 512, 1024
 QL = 256
 TINY = 1e-30
-G_RS, G_AG, P_SUB, P_ZR, P_XR, Z_RS, Y_AG, Y_B, S_RS, S_AG = range(10)
-STAGES = 10
+G_RS, G_AG, P_SUB, P_ZR, P_XR, Z_RS, Y_ZR, Y_XR, Y_B, S_RS, S_AG = range(11)
+STAGES = 11
 
 
 def dot(a, b, dims=((1,), (0,))):
@@ -234,7 +234,11 @@
     @pl.when(own_quarter)
     def _():
         yrt[feats, half] = total
-    to_plane(Y_AG, lambda o: ypiece, yct.at[feats, quarter])
+
+    def hand_product(i, carry):
+        push(Y_ZR, ypiece, yct.at[feats, quarter], x * NZ + lax.rem(z + i, NZ), c)
+        return carry
+    lax.fori_loop(1, NZ, hand_product, 0)
     yct[feats, quarter] = total
 
     def hand_across(i, carry):
@@ -248,6 +252,13 @@
     inv_row = jnp.broadcast_to(inv_scale, (B, 128)).T[0:1, :]
     inv_lower = inverse_factor(gram * inv_scale * inv_row)
     unscaled = inv_lower * inv_row
+    arrived(Y_ZR, first(zrecv, NZ - 1))
+
+    def hand_product_across(i, carry):
+        push(Y_XR, yct.at[:, quarter], yct.at[:, quarter], lax.rem(x + i, NX) * NZ + z, c)
+        return carry
+    lax.fori_loop(1, NX, hand_product_across, 0)
+
     basis_r = dot(unscaled, pt[...])
 
     arrived(S_RS, first(srecv, NG - 1))
@@ -259,7 +270,7 @@
     lax.fori_loop(1, NZ, send_rows_of_coupling, 0)
     sall[z] = sown[...]
 
-    arrived(Y_AG, first(zrecv, NR - 1))
+    arrived(Y_XR, yct.at[:, pl.ds(0, (NX - 1) * QL)])
     product_c = dot(inv_lower, yct[...])
 
     arrived(P_XR, ct.at[:, pl.ds(0, (NX - 1) * QL)])
@@ -293,7 +304,8 @@
     left(G_AG, first(gall, NR - 1))
     left(Z_RS, first(zrecv, NR - 1))
     left(P_XR, ct.at[:, pl.ds(0, (NX - 1) * QL)])
-    left(Y_AG, first(zrecv, NR - 1))
+    left(Y_ZR, first(zrecv, NZ - 1))
+    left(Y_XR, yct.at[:, pl.ds(0, (NX - 1) * QL)])
     left(P_ZR, first(zrecv, NZ - 1))
     left(S_RS, first(srecv, NG - 1))
     left(S_AG, first(sall, NZ - 1))

time: 47.2 us -> 45.6 us (0.966)
  Pallas kernels: 44.4 us -> 42.4 us
    pallas_call x1, Pallas kernels: 44.4 us -> 42.4 us  [local(): pl.pallas_call(panel_step, out_shape=(jax.ShapeDtypeStruct((RL, CL), F32)...]
where the time goes in v3:
time: 45.6 us; the launch traced here: 45 us
  Pallas kernels  42.4 us (93%)
  local copies, waits for them, and re-layouts  1.98 us (4%)
  between operations  0.64 us (1%)
    pallas_call x1, Pallas kernels, local(): pl.pallas_call(panel_step, out_shape=(jax.ShapeDtypeStruct((RL, CL), F32)...  42.4 us
    unnamed x2, local copies, waits for them, and re-layouts  1.98 us

profile of v3, /device:TPU:1, one launch (start us, length us, event | category | flops | bytes accessed | tf_op | source)
XLA Modules:
  0.0 45.0 jit_solution(7701247296161228634)
XLA Ops:
  0.6 42.4 %panel_step.1 = (f32[512,1024]{1,0:T(8,128)S(1)}, f32[64,512]{1,0:T(8,128)S(1)}) custom-call(f32[512,1024]{1,0:T(8,128)} %matrix_hbm.1, f32[64,512]{1,0:T(8,128)} %bitcast.3), custom_call_target="tpu_custom_call" | custom-call | tf_op jit(solution)/shard_map/panel_step/pallas_call | solution.py:333
  43.0 1.3 %copy.6 = f32[512,1024]{1,0:T(8,128)} copy(f32[512,1024]{1,0:T(8,128)S(1)} %get-tuple-element.8) | data formatting | bytes 4194304
  44.4 0.7 %copy.7 = f32[512,64]{0,1:T(8,128)} copy(f32[512,64]{0,1:T(8,128)S(1)} %bitcast.2) | data formatting | bytes 262144

commit v4 on v3

--- a/solution.py
+++ b/solution.py
@@ -72,7 +72,7 @@
     return work[:, B:] * root
 
 
-def panel_step(matrix_hbm, panel_hbm, out_ref, w_ref,
+def panel_step(matrix_hbm, panel_hbm, out_ref, w_ref, basis_ref, turned_ref,
                pt, zt, zrecv, gsend, grecv, gown, gall, ct, spart,
                ypiece, yct, yrt, ssend, srecv, sown, sall, in_sem, send_sem, recv_sem):
     r = lax.axis_index("row")
@@ -205,12 +205,18 @@
     spart[...] = scales * (1.0 / scale)
     share = spart[feats, :]
 
-    arrived(P_ZR, first(zrecv, NZ - 1))
     arrived(Z_RS, first(zrecv, NR - 1))
     total = zrecv[0] * share[:, 0:1]
     for k in range(1, NR):
         total = total + zrecv[k] * share[:, k:k + 1]
     ypiece[...] = total
+    def hand_product(i, carry):
+        push(Y_ZR, ypiece, yct.at[feats, quarter], x * NZ + lax.rem(z + i, NZ), c)
+        return carry
+    lax.fori_loop(1, NZ, hand_product, 0)
+    yct[feats, quarter] = total
+
+    arrived(P_ZR, first(zrecv, NZ - 1))
     part = dot(total, ct[:, quarter] * inv_scale, ((1,), (1,)))
     ssend[...] = jnp.concatenate([part[:4], part[4:]], axis=1)
 
@@ -234,12 +240,6 @@
     @pl.when(own_quarter)
     def _():
         yrt[feats, half] = total
-
-    def hand_product(i, carry):
-        push(Y_ZR, ypiece, yct.at[feats, quarter], x * NZ + lax.rem(z + i, NZ), c)
-        return carry
-    lax.fori_loop(1, NZ, hand_product, 0)
-    yct[feats, quarter] = total
 
     def hand_across(i, carry):
         push(P_XR, ct.at[:, quarter], ct.at[:, quarter], lax.rem(x + i, NX) * NZ + z, c)
@@ -295,10 +295,8 @@
     inner = jnp.concatenate([sall[k][:, h * B:(h + 1) * B] for k in range(NZ) for h in range(2)], axis=0)
     coupling = dot(dot(inv_lower, inner), inv_lower, ((1,), (1,)))
     w_ref[...] = 2.0 * product_r - 2.0 * dot(coupling, basis_r)
-    turned = 4.0 * dot(coupling, basis_c)
-    for t in range(RL // tile):
-        cols = pl.ds(t * tile, tile)
-        out_ref[cols, :] += dot3(basis_r[:, t * tile:(t + 1) * tile], turned)
+    turned_ref[...] = 4.0 * dot(coupling, basis_c)
+    basis_ref[...] = basis_r
 
     left(G_RS, first(gsend, NR - 1))
     left(G_AG, first(gall, NR - 1))
@@ -327,14 +325,30 @@
         left(P_SUB, first(zrecv, 16))
 
 
+def finish(part_ref, w_ref, basis_ref, turned_ref, out_hbm, w_hbm, out_v, sem, w_sem):
+    w_copy = pltpu.make_async_copy(w_ref, w_hbm, w_sem)
+    w_copy.start()
+    tile = 128
+    copies = []
+    for t in range(RL // tile):
+        rows = pl.ds(t * tile, tile)
+        out_v[rows, :] = part_ref[rows, :] + dot3(basis_ref[:, t * tile:(t + 1) * tile], turned_ref[...])
+        copies.append(pltpu.make_async_copy(out_v.at[rows], out_hbm.at[rows], sem.at[t]))
+        copies[-1].start()
+    for copy in copies:
+        copy.wait()
+    w_copy.wait()
+
+
 def local(matrix, panel):
     vmem = pl.BlockSpec(memory_space=pltpu.VMEM)
     in_hbm = pl.BlockSpec(memory_space=pltpu.HBM)
-    updated, weights = pl.pallas_call(
+    part, weights, basis, turned = pl.pallas_call(
         panel_step,
-        out_shape=(jax.ShapeDtypeStruct((RL, CL), F32), jax.ShapeDtypeStruct((B, RL), F32)),
+        out_shape=(jax.ShapeDtypeStruct((RL, CL), F32), jax.ShapeDtypeStruct((B, RL), F32),
+                   jax.ShapeDtypeStruct((B, RL), F32), jax.ShapeDtypeStruct((B, CL), F32)),
         in_specs=[in_hbm, in_hbm],
-        out_specs=(vmem, vmem),
+        out_specs=(vmem, vmem, vmem, vmem),
         scratch_shapes=[
             pltpu.VMEM((B, RL), F32),
             pltpu.VMEM((B, CL), F32),
@@ -358,6 +372,15 @@
             collective_id=0, has_side_effects=True, vmem_limit_bytes=24 << 20),
         name="panel_step",
     )(pltpu.with_memory_space_constraint(matrix, pltpu.HBM), pltpu.with_memory_space_constraint(panel.T, pltpu.HBM))
+    updated, weights = pl.pallas_call(
+        finish,
+        out_shape=(jax.ShapeDtypeStruct((RL, CL), F32), jax.ShapeDtypeStruct((B, RL), F32)),
+        in_specs=[vmem, vmem, vmem, vmem],
+        out_specs=(in_hbm, in_hbm),
+        scratch_shapes=[pltpu.VMEM((RL, CL), F32), pltpu.SemaphoreType.DMA((4,)), pltpu.SemaphoreType.DMA],
+        compiler_params=pltpu.CompilerParams(vmem_limit_bytes=24 << 20),
+        name="finish",
+    )(part, weights, basis, turned)
     return updated, weights.T
 
 

time: 45.6 us -> 44.4 us (0.974)
  local copies, waits for them, and re-layouts: 1.98 us -> 0 us
  Pallas kernels: 42.4 us -> 43.6 us
    unnamed x2 -> x0, local copies, waits for them, and re-layouts: 1.98 us -> none
    pallas_call x0 -> x1, Pallas kernels: none -> 1.71 us  [local(): pl.pallas_call(finish, out_shape=(jax.ShapeDtypeStruct((RL, CL), F32), ja...]
    pallas_call x1, Pallas kernels: 42.4 us -> 41.9 us  [local(): pl.pallas_call(panel_step, out_shape=(jax.ShapeDtypeStruct((RL, CL), F32)...]
where the time goes in v4:
time: 44.4 us; the launch traced here: 44.2 us
  Pallas kernels  43.6 us (98%)
  between operations  0.64 us (1%)
    pallas_call x1, Pallas kernels, local(): pl.pallas_call(panel_step, out_shape=(jax.ShapeDtypeStruct((RL, CL), F32)...  41.9 us
    pallas_call x1, Pallas kernels, local(): pl.pallas_call(finish, out_shape=(jax.ShapeDtypeStruct((RL, CL), F32), ja...  1.71 us

profile of v4, /device:TPU:1, one launch (start us, length us, event | category | flops | bytes accessed | tf_op | source)
XLA Modules:
  0.0 44.2 jit_solution(1482269033488619931)
XLA Ops:
  0.6 41.9 %panel_step.1 = (f32[512,1024]{1,0:T(8,128)S(1)}, f32[64,512]{1,0:T(8,128)S(1)}, f32[64,512]{1,0:T(8,128)S(1)}, f32[64,1024]{1,0:T(8,128)S(1)}) custom-call(f32[512,1024]{1,0:T(8,128)} %matrix_hbm.1, f32[64,512]{1,0:T(8,128)} %bitcast.2), custom_call_target="tpu_custom_call" | custom-call | tf_op jit(solution)/shard_map/panel_step/pallas_call | solution.py:346
  42.5 1.7 %finish.1 = (f32[512,1024]{1,0:T(8,128)}, f32[64,512]{1,0:T(8,128)}) custom-call(f32[512,1024]{1,0:T(8,128)S(1)} %get-tuple-element.8.part_ref, f32[64,512]{1,0:T(8,128)S(1)} %get-tuple-element.9.w_ref, f32[64,512]{1,0:T(8,128)S(1)} %get-tuple-element.10.basis_ref, f32[64,1024]{1,0:T(8,128)S(1)} %get-tuple-element.11.turned_ref), custom_call_target="tpu_custom_call" | custom-call | tf_op jit(solution)/shard_map/finish/pallas_call | solution.py:375

commit v5 on v4

--- a/solution.py
+++ b/solution.py
@@ -242,7 +242,7 @@
         yrt[feats, half] = total
 
     def hand_across(i, carry):
-        push(P_XR, ct.at[:, quarter], ct.at[:, quarter], lax.rem(x + i, NX) * NZ + z, c)
+        push(P_XR, ct.at[:, quarter], ct.at[:, quarter], lax.rem(x + 1 + lax.rem(i, 3), NX) * NZ + z, c)
         return carry
     lax.fori_loop(1, NX, hand_across, 0)
 
@@ -255,7 +255,7 @@
     arrived(Y_ZR, first(zrecv, NZ - 1))
 
     def hand_product_across(i, carry):
-        push(Y_XR, yct.at[:, quarter], yct.at[:, quarter], lax.rem(x + i, NX) * NZ + z, c)
+        push(Y_XR, yct.at[:, quarter], yct.at[:, quarter], lax.rem(x + 1 + lax.rem(i, 3), NX) * NZ + z, c)
         return carry
     lax.fori_loop(1, NX, hand_product_across, 0)
 

time: 44.4 us -> 44.4 us (level)
  no operation moved by 1% of the time
where the time goes in v5:
time: 44.4 us; the launch traced here: 44.2 us
  Pallas kernels  43.6 us (98%)
  between operations  0.64 us (1%)
    pallas_call x1, Pallas kernels, local(): pl.pallas_call(panel_step, out_shape=(jax.ShapeDtypeStruct((RL, CL), F32)...  41.9 us
    pallas_call x1, Pallas kernels, local(): pl.pallas_call(finish, out_shape=(jax.ShapeDtypeStruct((RL, CL), F32), ja...  1.71 us

profile of v5, /device:TPU:1, one launch (start us, length us, event | category | flops | bytes accessed | tf_op | source)
XLA Modules:
  0.0 44.2 jit_solution(10212595149203601637)
XLA Ops:
  0.6 41.9 %panel_step.1 = (f32[512,1024]{1,0:T(8,128)S(1)}, f32[64,512]{1,0:T(8,128)S(1)}, f32[64,512]{1,0:T(8,128)S(1)}, f32[64,1024]{1,0:T(8,128)S(1)}) custom-call(f32[512,1024]{1,0:T(8,128)} %matrix_hbm.1, f32[64,512]{1,0:T(8,128)} %bitcast.2), custom_call_target="tpu_custom_call" | custom-call | tf_op jit(solution)/shard_map/panel_step/pallas_call | solution.py:346
  42.5 1.7 %finish.1 = (f32[512,1024]{1,0:T(8,128)}, f32[64,512]{1,0:T(8,128)}) custom-call(f32[512,1024]{1,0:T(8,128)S(1)} %get-tuple-element.8.part_ref, f32[64,512]{1,0:T(8,128)S(1)} %get-tuple-element.9.w_ref, f32[64,512]{1,0:T(8,128)S(1)} %get-tuple-element.10.basis_ref, f32[64,1024]{1,0:T(8,128)S(1)} %get-tuple-element.11.turned_ref), custom_call_target="tpu_custom_call" | custom-call | tf_op jit(solution)/shard_map/finish/pallas_call | solution.py:375
